TPU v7x, 32 devices: a whole 2x2x4 slice. The times are simulated.
32 devices in a mesh: band: 8 (over z, y), mp: 4 (over x, core).
Axes of the slice: x: 2, y: 2, z: 4, core: 2. Of those that a mesh axis runs over, the one named last changes fastest.
Arguments:
- cells: bfloat16 [2048, 1024], P('band', 'mp'), may hold values from -81 to 81
- row_gain: float32 [1024], replicated, may hold values from 0.1 to 1.9
- row_qkv: bfloat16 [3, 1024, 1024], P(None, None, 'mp'), may hold values from -1.25 to 1.25
- row_out: bfloat16 [1024, 1024], P('mp'), may hold values from -0.1875 to 0.1875
- col_gain: float32 [1024], replicated, may hold values from 0.1 to 1.9
- col_qkv: bfloat16 [3, 1024, 1024], P(None, None, 'mp'), may hold values from -1.25 to 1.25
- col_out: bfloat16 [1024, 1024], P('mp'), may hold values from -0.1875 to 0.1875
- row_seg: int32 [2048], P('band'), may hold values from 0 to 255, never falling along the last dimension, each value on 1 to 16 neighbouring positions
- col_dest: int32 [2048, 1], P('band'), may hold values from 0 to 7; in each aligned block of 256 rows (0 to 255, 256 to 511, ...) at most 48 rows name the same one
- sheet_column_index: int32 [2048], P('band'), may hold values from 1 to 8
- d_result: bfloat16 [2048, 1024], P('band', 'mp'), may hold values from -6 to 6
Outputs:
- result: bfloat16 [2048, 1024], P('band', 'mp')
- d_cells: bfloat16 [2048, 1024], P('band', 'mp')
Inputs may be any that keep to these rules, and one draw needn't show every extreme that they name: `row_seg`: cells never fall in value along the array. `col_dest`: at most 48 of the cells of one row band name the same column band, and some row band sends exactly 48 to some column band.
All inputs are finite; a program needn't handle non-finite values.
Results may differ from a plain program's by a relative error of at most 0.019.
Values may be sent and summed in bfloat16 or wider, within the bound.
A program may use at most 64 MiB of HBM per device.

v0:
```python
import jax
import jax.numpy as jnp
from jax import lax
from jax.sharding import PartitionSpec as P

HEAD_DIM = 64
TILE = 128
norm_eps = 1e-06
neg_fill = -1e30


def block_terms(inputs, norm_gain, query_key_value_weight, w_out, allowed, tile_rows):
    values = inputs.astype(jnp.float32)
    inv_rms = lax.rsqrt(jnp.mean(values * values, axis=-1, keepdims=True) + norm_eps)
    normalized_cells = (values * inv_rms * norm_gain).astype(jnp.bfloat16)
    projected_heads = jnp.einsum(
        "lu,xuh->xlh", normalized_cells, query_key_value_weight, preferred_element_type=jnp.float32
    ).astype(jnp.bfloat16)
    row_count = inputs.shape[0]
    feat_width = query_key_value_weight.shape[2]
    head_count = feat_width // HEAD_DIM
    shaped = projected_heads.reshape(3, row_count // tile_rows, tile_rows, head_count, HEAD_DIM)
    scores = jnp.einsum(
        "bqhe,bkhe->bhqk", shaped[0], shaped[1], preferred_element_type=jnp.float32
    ) * HEAD_DIM ** (-0.5)
    scores = jnp.where(allowed[:, None], scores, neg_fill)
    scores = scores - lax.stop_gradient(jnp.max(scores, axis=-1, keepdims=True))
    expd = jnp.exp(scores)
    attn_probs = (expd / jnp.sum(expd, axis=-1, keepdims=True)).astype(jnp.bfloat16)
    attended = jnp.einsum(
        "bhqk,bkhe->bqhe", attn_probs, shaped[2], preferred_element_type=jnp.float32
    ).astype(jnp.bfloat16)
    attended = attended.reshape(row_count, feat_width)
    return jnp.dot(attended, w_out, preferred_element_type=jnp.float32)


def column_band_mask(col_keys):
    positions = jnp.arange(col_keys.shape[0])
    same_col = (col_keys[:, None] == col_keys[None, :]) & (col_keys[None, :] > 0)
    return (same_col | (positions[:, None] == positions[None, :]))[None]


def widen(block):
    return lax.all_gather(block, "mp", axis=1, tiled=True)


def narrow(terms):
    return lax.psum_scatter(
        terms.astype(jnp.bfloat16), "mp", scatter_dimension=1, tiled=True
    ).astype(jnp.float32)


def move_rows(rows):
    return lax.all_to_all(rows, "band", split_axis=0, concat_axis=0, tiled=True)


def on_device(
    cells,
    row_gain,
    row_qkv,
    row_out,
    col_gain,
    col_qkv,
    col_out,
    row_seg,
    col_dest,
    sheet_column_index,
    d_result,
):
    cell_rows, feat_width = cells.shape
    band_count = lax.axis_size("band")
    capacity = max(2, 3 * cell_rows // (2 * band_count))
    slot_total = band_count * capacity
    gathered = widen(cells)
    row_groups = row_seg.reshape(cell_rows // TILE, TILE)
    row_mask = row_groups[:, :, None] == row_groups[:, None, :]

    def row_local(inputs):
        return block_terms(inputs, row_gain, row_qkv, row_out, row_mask, TILE)

    row_terms, row_pull = jax.vjp(row_local, gathered)
    target = col_dest[:, 0]
    place = jnp.arange(cell_rows, dtype=jnp.int32)
    earlier = (target[:, None] == target[None, :]) & (place[None, :] < place[:, None])
    ranking = jnp.sum(earlier.astype(jnp.int32), axis=1)
    slot_index = target * capacity + ranking
    keys_out = (
        jnp.zeros((slot_total,), jnp.bfloat16)
        .at[slot_index]
        .set(sheet_column_index.astype(jnp.bfloat16))
    )
    back_in = jnp.zeros((slot_total, feat_width), jnp.bfloat16).at[slot_index].set(d_result)
    mixed_rows = (cells.astype(jnp.float32) + narrow(row_terms)).astype(jnp.bfloat16)
    outgoing = jnp.zeros((slot_total, feat_width), jnp.bfloat16).at[slot_index].set(mixed_rows)
    arrived, col_keys = (
        lax.all_to_all(outgoing, "band", split_axis=0, concat_axis=0, tiled=True),
        lax.all_to_all(keys_out, "band", split_axis=0, concat_axis=0, tiled=True),
    )
    column_full = widen(arrived)
    col_allowed = column_band_mask(col_keys)

    def col_local(inputs):
        return block_terms(inputs, col_gain, col_qkv, col_out, col_allowed, inputs.shape[0])

    col_terms, col_pull = jax.vjp(col_local, column_full)
    settled = (arrived.astype(jnp.float32) + narrow(col_terms)).astype(jnp.bfloat16)
    result = move_rows(settled)[slot_index]
    d_column = move_rows(back_in)
    (d_col_part,) = col_pull(widen(d_column).astype(jnp.float32))
    d_mixed_col = (d_column.astype(jnp.float32) + narrow(d_col_part.astype(jnp.float32))).astype(
        jnp.bfloat16
    )
    d_mixed = move_rows(d_mixed_col)[slot_index]
    (d_row_part,) = row_pull(widen(d_mixed).astype(jnp.float32))
    d_cells = (d_mixed.astype(jnp.float32) + narrow(d_row_part.astype(jnp.float32))).astype(
        jnp.bfloat16
    )
    return (result, d_cells)


def solution(mesh):
    in_specs = (
        P("band", "mp"),
        P(),
        P(None, None, "mp"),
        P("mp", None),
        P(),
        P(None, None, "mp"),
        P("mp", None),
        P("band"),
        P("band", None),
        P("band"),
        P("band", "mp"),
    )
    out_specs = (P("band", "mp"), P("band", "mp"))
    return jax.shard_map(
        on_device, mesh=mesh, in_specs=in_specs, out_specs=out_specs, check_vma=False
    )
```

profile of v0, /device:TPU:0, one launch (start us, length us, event | category | flops | bytes accessed | tf_op | source)
XLA Modules:
  0.0 187.2 jit_solution(12250987462010092255)
XLA Ops:
  7.2 9.0 %all_gather.12 = bf16[256,1024]{1,0:T(8,128)(2,1)S(1)} all-gather(bf16[256,256]{1,0:T(8,128)(2,1)} %param.11), channel_id=1, replica_groups=mesh['band'=8,'mp'=4] {'mp'}, dimensions={1}, use_global_device_ids=true | all-gather | bytes 655360 | tf_op jit(solution)/shard_map/all_gather | solution.py:44
  16.4 2.1 %fusion.21 = bf16[3,256,256]{2,1,0:T(8,128)(2,1)S(1)} fusion(bf16[3,1024,256]{2,1,0:T(8,128)(2,1)} %param.13, bf16[256,1024]{1,0:T(8,128)(2,1)S(1)} %all_gather.12, f32[1024]{0:T(1024)} %param.12, f32[256]{0:T(256)S(1)} %fusion.61), kind=kOutput, calls=%fused_computation.50 | convolution fusion | flops 403898368 | bytes 2495488 | tf_op jit(solution)/shard_map/jvp(lu,xuh->xlh)/dot_general | solution.py:16
  23.7 2.2 %scatter_custom_fusion.1 = bf16[384]{0:T(512)(128)(2,1)S(1)} fusion(s32[256]{0:T(256)S(1)} %bitcast.155, bf16[256]{0:T(256)(128)(2,1)S(1)} %convert_element_type.204, bf16[]{:T(256)} %constant.12.clone.1), kind=kCustom, calls=%fused_computation.121 | custom fusion | bytes 770 | tf_op jit(solution)/shard_map/scatter | solution.py:90
  26.5 5.8 %all-to-all-start.1 = ((bf16[8,48,1]{1,2,0:T(2,128)(2,1)}), bf16[8,48,1]{1,2,0:T(2,128)(2,1)S(1)}, u32[]{:S(2)}, u32[]{:S(2)}) async-start(bf16[8,48,1]{1,2,0:T(2,128)(2,1)} %all_to_all.52), calls=%async_computation.2 | async-start | bytes 8192 | tf_op jit(solution)/shard_map/all_to_all | solution.py:97
  32.4 2.5 %scatter_custom_fusion.2 = bf16[384,256]{1,0:T(8,128)(2,1)} fusion(s32[256]{0:T(256)S(1)} %bitcast.156, bf16[256,256]{1,0:T(8,128)(2,1)} %param.21, bf16[]{:T(256)} %constant.12.clone.1), kind=kCustom, calls=%fused_computation.106 | custom fusion | bytes 197120 | tf_op jit(solution)/shard_map/scatter | solution.py:92
  34.8 4.0 %all-to-all-done.1 = bf16[8,48,1]{1,2,0:T(2,128)(2,1)S(1)} async-done(((bf16[8,48,1]{1,2,0:T(2,128)(2,1)}), bf16[8,48,1]{1,2,0:T(2,128)(2,1)S(1)}, u32[]{:S(2)}, u32[]{:S(2)}) %all-to-all-start.1) | async-done | bytes 800 | tf_op jit(solution)/shard_map/all_to_all | solution.py:97
  38.8 3.4 %all-to-all-start.3 = ((bf16[8,48,256]{2,1,0:T(8,128)(2,1)}), bf16[8,48,256]{2,1,0:T(8,128)(2,1)S(1)}, u32[]{:S(2)}, u32[]{:S(2)}) async-start(bf16[8,48,256]{2,1,0:T(8,128)(2,1)} %bitcast.19), calls=%async_computation.5 | async-start | bytes 393216 | tf_op jit(solution)/shard_map/all_to_all | solution.py:54
  43.2 2.9 %reduce-scatter.5.cloned.1.call-done = bf16[256,256]{1,0:T(8,128)(2,1)} async-done(((bf16[256,1024]{1,0:T(8,128)(2,1)}), bf16[256,256]{1,0:T(8,128)(2,1)}) %reduce-scatter.5.cloned.1.call-update) | async-done | bytes 131088 | tf_op jit(solution)/shard_map/reduce_scatter | solution.py:48
  46.1 2.5 %scatter_custom_fusion = bf16[384,256]{1,0:T(8,128)(2,1)} fusion(s32[256]{0:T(256)S(1)} %bitcast.157, bf16[256,256]{1,0:T(8,128)(2,1)} %reduce-scatter.5.cloned.1.call-done, bf16[256,256]{1,0:T(8,128)(2,1)S(1)} %copy-done.12, bf16[]{:T(256)} %constant.12.clone.1), kind=kCustom, calls=%fused_computation.101 | custom fusion | flops 262144 | bytes 458754 | tf_op jit(solution)/shard_map/scatter | solution.py:94
  50.0 4.3 %all-to-all-start = ((bf16[8,48,256]{2,1,0:T(8,128)(2,1)}), bf16[8,48,256]{2,1,0:T(8,128)(2,1)S(1)}, u32[]{:S(2)}, u32[]{:S(2)}) async-start(bf16[8,48,256]{2,1,0:T(8,128)(2,1)} %bitcast.7), calls=%async_computation.1 | async-start | bytes 393216 | tf_op jit(solution)/shard_map/all_to_all | solution.py:96
  54.3 7.9 %all_gather.14 = bf16[384,1024]{1,0:T(8,128)(2,1)S(1)} all-gather(bf16[384,256]{1,0:T(8,128)(2,1)S(1)} %bitcast.137), channel_id=1, replica_groups=mesh['band'=8,'mp'=4] {'mp'}, dimensions={1}, use_global_device_ids=true | all-gather | bytes 983040 | tf_op jit(solution)/shard_map/all_gather | solution.py:44
  62.7 8.9 %all_gather.13 = bf16[384,1024]{1,0:T(8,128)(2,1)S(1)} all-gather(bf16[384,256]{1,0:T(8,128)(2,1)S(1)} %bitcast.136), channel_id=1, replica_groups=mesh['band'=8,'mp'=4] {'mp'}, dimensions={1}, use_global_device_ids=true | all-gather | bytes 983040 | tf_op jit(solution)/shard_map/all_gather | solution.py:44
  73.8 3.5 %fusion.74 = (f32[4,384]{1,0:T(4,128)S(1)}, f32[4,384,384]{1,2,0:T(8,128)}) fusion(pred[384,384]{0,1:T(8,128)(4,1)} %fusion.43, bf16[384,4,64]{0,2,1:T(8,128)(2,1)} %bitcast.150, bf16[384,4,64]{0,2,1:T(8,128)(2,1)} %bitcast.147), kind=kOutput, calls=%fused_computation.131 | convolution fusion | flops 77857152 | bytes 2906112 | tf_op jit(solution)/shard_map/jvp()/sub | solution.py:27
  77.4 3.7 %fusion.7 = (f32[4,384]{1,0:T(4,128)S(1)}, bf16[4,384,384]{1,2,0:T(8,128)(2,1)}, bf16[4,384,384]{1,2,0:T(8,128)(2,1)}) fusion(f32[4,384,384]{1,2,0:T(8,128)} %get-tuple-element.13, f32[4,384]{1,0:T(4,128)S(1)} %multiply_divide_fusion, f32[4,384]{1,0:T(4,128)S(1)} %get-tuple-element.12, bf16[4,64,384]{2,1,0:T(8,128)(2,1)S(1)} %bitcast.141, ...), kind=kOutput, calls=%fused_computation.19 | convolution fusion | flops 79624704 | bytes 5130240 | tf_op jit(solution)/shard_map/transpose(jvp(bhqk,bkhe->bqhe))/dot_general | solution.py:30
  81.1 3.9 %fusion.26 = bf16[1,1,384,4,64]{2,4,3,1,0:T(8,128)(2,1)} fusion(bf16[384,4,64]{0,2,1:T(8,128)(2,1)} %bitcast.151, bf16[4,384,384]{1,2,0:T(8,128)(2,1)} %get-tuple-element.14, f32[4,384]{1,0:T(4,128)S(1)} %neg.13, f32[4,384]{1,0:T(4,128)S(1)} %get-tuple-element.12, pred[384,384]{0,1:T(8,128)(4,1)} %fusion.43, bf16[384,4,64]{0,2,1:T(8,128)(2,1)S(1)} %bitcast.148), kind=kOutput, calls=%fused_computation.61 | convolution fusion | flops 156403584 | bytes 1929216 | tf_op jit(solution)/shard_map/transpose(jvp(bqhe,bkhe->bhqk))/dot_general | solution.py:23
  85.0 3.6 %fusion.27 = bf16[1,1,384,4,64]{2,4,3,1,0:T(8,128)(2,1)} fusion(bf16[384,4,64]{0,2,1:T(8,128)(2,1)S(1)} %bitcast.149, bf16[4,384,384]{1,2,0:T(8,128)(2,1)} %get-tuple-element.14, f32[4,384]{1,0:T(4,128)S(1)} %neg.13, f32[4,384]{1,0:T(4,128)S(1)} %get-tuple-element.12, pred[384,384]{0,1:T(8,128)(4,1)} %fusion.43, bf16[384,4,64]{0,2,1:T(8,128)(2,1)S(1)} %bitcast.152), kind=kOutput, calls=%fused_computation.62 | convolution fusion | flops 156403584 | bytes 1929216 | tf_op jit(solution)/shard_map/transpose(jvp(bqhe,bkhe->bhqk))/dot_general | solution.py:23
  96.0 24.5 %reduce-scatter.9.cloned.1.call-done = bf16[384,256]{1,0:T(8,128)(2,1)} async-done(((bf16[384,1024]{1,0:T(8,128)(2,1)}), bf16[384,256]{1,0:T(8,128)(2,1)}) %reduce-scatter.9.cloned.1.call-update) | async-done | bytes 196624 | tf_op jit(solution)/shard_map/reduce_scatter | solution.py:48
  122.2 5.5 %all-to-all-start.4 = ((bf16[8,48,256]{2,1,0:T(8,128)(2,1)}), bf16[8,48,256]{2,1,0:T(8,128)(2,1)S(1)}, u32[]{:S(2)}, u32[]{:S(2)}) async-start(bf16[8,48,256]{2,1,0:T(8,128)(2,1)} %bitcast.38), calls=%async_computation.7 | async-start | bytes 393216 | tf_op jit(solution)/shard_map/all_to_all | solution.py:54
  130.9 4.8 %all-to-all-done.4 = bf16[8,48,256]{2,1,0:T(8,128)(2,1)S(1)} async-done(((bf16[8,48,256]{2,1,0:T(8,128)(2,1)}), bf16[8,48,256]{2,1,0:T(8,128)(2,1)S(1)}, u32[]{:S(2)}, u32[]{:S(2)}) %all-to-all-start.4) | async-done | bytes 196640 | tf_op jit(solution)/shard_map/all_to_all | solution.py:54
  136.9 6.7 %all-gather = bf16[256,1024]{1,0:T(8,128)(2,1)S(1)} all-gather(bf16[256,256]{1,0:T(8,128)(2,1)S(1)} %gather_fusion.1), channel_id=2, replica_groups=mesh['band'=8,'mp'=4] {'mp'}, dimensions={1}, use_global_device_ids=true | all-gather | bytes 655360 | tf_op jit(solution)/shard_map/all_gather | solution.py:44
  148.2 2.2 %fusion.37 = (f32[256]{0:T(256)S(1)}, f32[256,1024]{1,0:T(8,128)S(1)}) fusion(bf16[256,1024]{1,0:T(8,128)(2,1)S(1)} %all_gather.12, f32[1024]{0:T(1024)S(1)} %copy-done.21, bf16[3,1024,256]{2,1,0:T(8,128)(2,1)} %param.13, bf16[3,256,256]{1,2,0:T(8,128)(2,1)S(1)} %reshape.262), kind=kOutput, calls=%fused_computation.77 | convolution fusion | flops 404225792 | bytes 3544064 | tf_op jit(solution)/shard_map/transpose(jvp(lu,xuh->xlh))/dot_general | solution.py:16
  151.4 3.5 %reduce-scatter.7.cloned.1.call-done = bf16[384,256]{1,0:T(8,128)(2,1)} async-done(((bf16[384,1024]{1,0:T(8,128)(2,1)}), bf16[384,256]{1,0:T(8,128)(2,1)}) %reduce-scatter.7.cloned.1.call-update) | async-done | bytes 196624 | tf_op jit(solution)/shard_map/reduce_scatter | solution.py:48
  155.9 13.2 %all_to_all.58 = bf16[8,48,256]{2,1,0:T(8,128)(2,1)S(1)} all-to-all(bf16[8,48,256]{2,1,0:T(8,128)(2,1)S(1)} %bitcast.140), channel_id=1, replica_groups=mesh['band'=8,'mp'=4] {'band'}, dimensions={0} | all-to-all | bytes 393216 | tf_op jit(solution)/shard_map/all_to_all | solution.py:54
  171.0 8.2 %reduce-scatter.11.cloned.1.call-done = bf16[256,256]{1,0:T(8,128)(2,1)} async-done(((bf16[256,1024]{1,0:T(8,128)(2,1)}), bf16[256,256]{1,0:T(8,128)(2,1)}) %reduce-scatter.11.cloned.1.call-update) | async-done | bytes 131088 | tf_op jit(solution)/shard_map/reduce_scatter | solution.py:48
  (115 shorter events, 34.1 us)
Async XLA Ops:
  7.2 64.7 %copy-start = (bf16[3,1024,256]{2,1,0:T(8,128)(2,1)S(1)}, bf16[3,1024,256]{2,1,0:T(8,128)(2,1)}, u32[]{:S(2)}) copy-start(bf16[3,1024,256]{2,1,0:T(8,128)(2,1)} %param.16) | copy-start | bytes 4718596
  7.2 39.0 %reduce-scatter.5.cloned.1.call-start = ((), (), s32[]{:S(2)}) async-start(), calls=%async_computation.9 | async-start | bytes 655360 | tf_op jit(solution)/shard_map/reduce_scatter | solution.py:48
  19.0 3.3 %copy-start.3 = (bf16[256,1024]{1,0:T(8,128)(2,1)S(1)}, bf16[256,1024]{1,0:T(8,128)(2,1)}, u32[]{:S(2)}) copy-start(bf16[256,1024]{1,0:T(8,128)(2,1)} %param.14) | copy-start | bytes 1572868
  19.6 3.8 %copy-start.23 = (s32[256]{0:T(256)S(1)}, s32[256]{0:T(256)}, u32[]{:S(2)}) copy-start(s32[256]{0:T(256)} %param.20) | copy-start | bytes 3076
  19.7 3.8 %copy-start.19 = (s32[256,1]{0,1:T(1,128)S(1)}, s32[256,1]{0,1:T(1,128)}, u32[]{:S(2)}) copy-start(s32[256,1]{0,1:T(1,128)} %param.19) | copy-start | bytes 3076
  20.9 25.3 %copy-start.12 = (bf16[256,256]{1,0:T(8,128)(2,1)S(1)}, bf16[256,256]{1,0:T(8,128)(2,1)}, u32[]{:S(2)}) copy-start(bf16[256,256]{1,0:T(8,128)(2,1)} %param.11) | copy-start | bytes 393220
  22.2 40.1 %copy-start.1 = (bf16[256,1024]{1,0:T(8,128)(2,1)S(1)}, bf16[256,1024]{1,0:T(8,128)(2,1)}, u32[]{:S(2)}) copy-start(bf16[256,1024]{1,0:T(8,128)(2,1)} %param.17) | copy-start | bytes 1572868
  26.5 12.3 %all-to-all-start.1 = ((bf16[8,48,1]{1,2,0:T(2,128)(2,1)}), bf16[8,48,1]{1,2,0:T(2,128)(2,1)S(1)}, u32[]{:S(2)}, u32[]{:S(2)}) async-start(bf16[8,48,1]{1,2,0:T(2,128)(2,1)} %all_to_all.52), calls=%async_computation.2 | async-start | bytes 8192 | tf_op jit(solution)/shard_map/all_to_all | solution.py:97
  38.8 11.1 %all-to-all-start.3 = ((bf16[8,48,256]{2,1,0:T(8,128)(2,1)}), bf16[8,48,256]{2,1,0:T(8,128)(2,1)S(1)}, u32[]{:S(2)}, u32[]{:S(2)}) async-start(bf16[8,48,256]{2,1,0:T(8,128)(2,1)} %bitcast.19), calls=%async_computation.5 | async-start | bytes 393216 | tf_op jit(solution)/shard_map/all_to_all | solution.py:54
  48.6 23.3 %copy-start.20 = (f32[1024]{0:T(1024)S(1)}, f32[1024]{0:T(1024)}, u32[]{:S(2)}) copy-start(f32[1024]{0:T(1024)} %param.15) | copy-start | bytes 12292
  50.0 12.8 %copy-start.7 = (bf16[8,48,256]{2,1,0:T(8,128)(2,1)}, bf16[8,48,256]{2,1,0:T(8,128)(2,1)S(1)}, u32[]{:S(2)}) copy-start(bf16[8,48,256]{2,1,0:T(8,128)(2,1)S(1)} %all-to-all-done.3) | copy-start | bytes 589828
  50.0 12.7 %all-to-all-start = ((bf16[8,48,256]{2,1,0:T(8,128)(2,1)}), bf16[8,48,256]{2,1,0:T(8,128)(2,1)S(1)}, u32[]{:S(2)}, u32[]{:S(2)}) async-start(bf16[8,48,256]{2,1,0:T(8,128)(2,1)} %bitcast.7), calls=%async_computation.1 | async-start | bytes 393216 | tf_op jit(solution)/shard_map/all_to_all | solution.py:96
  54.3 66.2 %reduce-scatter.9.cloned.1.call-start = ((), (), s32[]{:S(2)}) async-start(), calls=%async_computation.11 | async-start | bytes 983040 | tf_op jit(solution)/shard_map/reduce_scatter | solution.py:48
  62.7 10.3 %copy-start.5 = (bf16[8,48,256]{2,1,0:T(8,128)(2,1)}, bf16[8,48,256]{2,1,0:T(8,128)(2,1)S(1)}, u32[]{:S(2)}) copy-start(bf16[8,48,256]{2,1,0:T(8,128)(2,1)S(1)} %all-to-all-done) | copy-start | bytes 589828
  73.8 7.3 %copy-start.8 = (bf16[1,384,256]{1,2,0:T(8,128)(2,1)}, bf16[1,384,256]{1,2,0:T(8,128)(2,1)S(1)}, u32[]{:S(2)}) copy-start(bf16[1,384,256]{1,2,0:T(8,128)(2,1)S(1)} %get-tuple-element.6) | copy-start | bytes 589828
  77.4 3.7 %copy-start.13 = (bf16[1,384,256]{1,2,0:T(8,128)(2,1)S(1)}, bf16[1,384,256]{1,2,0:T(8,128)(2,1)}, u32[]{:S(2)}) copy-start(bf16[1,384,256]{1,2,0:T(8,128)(2,1)} %get-tuple-element.4) | copy-start | bytes 589828
  81.1 3.9 %copy-start.14 = (bf16[1,384,256]{1,2,0:T(8,128)(2,1)S(1)}, bf16[1,384,256]{1,2,0:T(8,128)(2,1)}, u32[]{:S(2)}) copy-start(bf16[1,384,256]{1,2,0:T(8,128)(2,1)} %get-tuple-element.5) | copy-start | bytes 589828
  94.7 34.9 %copy-start.2 = (bf16[256,1024]{1,0:T(8,128)(2,1)S(1)}, bf16[256,1024]{1,0:T(8,128)(2,1)}, u32[]{:S(2)}) copy-start(bf16[256,1024]{1,0:T(8,128)(2,1)} %param.17) | copy-start | bytes 1572868
  122.2 13.5 %all-to-all-start.4 = ((bf16[8,48,256]{2,1,0:T(8,128)(2,1)}), bf16[8,48,256]{2,1,0:T(8,128)(2,1)S(1)}, u32[]{:S(2)}, u32[]{:S(2)}) async-start(bf16[8,48,256]{2,1,0:T(8,128)(2,1)} %bitcast.38), calls=%async_computation.7 | async-start | bytes 393216 | tf_op jit(solution)/shard_map/all_to_all | solution.py:54
  127.8 27.2 %reduce-scatter.7.cloned.1.call-start = ((), (), s32[]{:S(2)}) async-start(), calls=%async_computation.10 | async-start | bytes 983040 | tf_op jit(solution)/shard_map/reduce_scatter | solution.py:48
  129.5 14.1 %copy-start.4 = (bf16[256,1024]{1,0:T(8,128)(2,1)S(1)}, bf16[256,1024]{1,0:T(8,128)(2,1)}, u32[]{:S(2)}) copy-start(bf16[256,1024]{1,0:T(8,128)(2,1)} %param.14) | copy-start | bytes 1572868
  130.8 13.3 %copy-start.10 = (bf16[2,128,4,64]{1,3,2,0:T(8,128)(2,1)S(1)}, bf16[2,128,4,64]{1,3,2,0:T(8,128)(2,1)}, u32[]{:S(2)}) copy-start(bf16[2,128,4,64]{1,3,2,0:T(8,128)(2,1)} %copy-done.9) | copy-start | bytes 393220
  130.8 48.3 %reduce-scatter.11.cloned.1.call-start = ((), (), s32[]{:S(2)}) async-start(), calls=%async_computation.12 | async-start | bytes 655360 | tf_op jit(solution)/shard_map/reduce_scatter | solution.py:48
  148.2 6.8 %copy-start.6 = (bf16[8,48,256]{2,1,0:T(8,128)(2,1)S(1)}, bf16[8,48,256]{2,1,0:T(8,128)(2,1)}, u32[]{:S(2)}) copy-start(bf16[8,48,256]{2,1,0:T(8,128)(2,1)} %copy-done.5) | copy-start | bytes 589828
  (8 other events, 15.4 us)
Sparse Core Ops, SparseCore 0:
  23.6 22.5 reduce-scatter.4
  96.1 24.3 reduce-scatter.8
  131.1 23.7 reduce-scatter.6
  157.4 21.6 reduce-scatter.10
where the time goes:
time: 188 us; the launch traced here: 187 us
  waiting for transfers between devices  49.3 us (26%)
  blocking collectives  45.7 us (24%)
  matrix products  34.5 us (18%)
  starting transfers between devices  19.2 us (10%)
  between operations  14.3 us (8%)
  local copies, waits for them, and re-layouts  12.3 us (7%)
  other arithmetic  11.9 us (6%)
    reduce_scatter x4, waiting for transfers between devices, narrow(): lax.psum_scatter(terms.astype(jnp.bfloat16), 'mp', scatter_dimension=1, t...  39.1 us
    all_gather x4, blocking collectives, widen(): return lax.all_gather(block, 'mp', axis=1, tiled=True)  32.5 us
    all_to_all x1, blocking collectives, move_rows(): return lax.all_to_all(rows, 'band', split_axis=0, concat_axis=0, tiled=True)  13.2 us
    dot_general x6, matrix products, block_terms(): jnp.einsum('bhqk,bkhe->bqhe', attn_probs, shaped[2], preferred_element_ty...  11.2 us
    all_to_all x2, starting transfers between devices, move_rows(): return lax.all_to_all(rows, 'band', split_axis=0, concat_axis=0, tiled=True)  8.92 us
    dot_general x4, matrix products, block_terms(): jnp.einsum('bqhe,bkhe->bhqk', shaped[0], shaped[1], preferred_element_typ...  8.12 us
    dot_general x4, matrix products, block_terms(): jnp.einsum('lu,xuh->xlh', normalized_cells, query_key_value_weight, prefe...  7.29 us
    all_to_all x2, waiting for transfers between devices, move_rows(): return lax.all_to_all(rows, 'band', split_axis=0, concat_axis=0, tiled=True)  6.16 us
  transfers between devices with their start and end apart: 8, of which 7 were waited for; matrix products, arithmetic and copies ran while one was open for 12% of the time, Pallas kernels for 0%

commit v1 on v0

--- a/solution.py
+++ b/solution.py
@@ -7,6 +7,22 @@
 TILE = 128
 norm_eps = 1e-06
 neg_fill = -1e30
+
+
+def exchange_in_pairs(array, axis, split, join):
+    ways, here = (lax.axis_size(axis), lax.axis_index(axis))
+    width = array.shape[split] // ways
+    shape = list(array.shape)
+    shape[split] = width
+    height = shape[join]
+    shape[join] = height * ways
+    full = jnp.zeros(shape, array.dtype)
+    for mask in range(ways):
+        part = lax.dynamic_slice_in_dim(array, (here ^ mask) * width, width, axis=split)
+        if mask:
+            part = lax.ppermute(part, axis, [(d, d ^ mask) for d in range(ways)])
+        full = lax.dynamic_update_slice_in_dim(full, part, (here ^ mask) * height, axis=join)
+    return full
 
 
 def block_terms(inputs, norm_gain, query_key_value_weight, w_out, allowed, tile_rows):
@@ -93,7 +109,7 @@
     mixed_rows = (cells.astype(jnp.float32) + narrow(row_terms)).astype(jnp.bfloat16)
     outgoing = jnp.zeros((slot_total, feat_width), jnp.bfloat16).at[slot_index].set(mixed_rows)
     arrived, col_keys = (
-        lax.all_to_all(outgoing, "band", split_axis=0, concat_axis=0, tiled=True),
+        exchange_in_pairs(outgoing, "band", 0, 0),
         lax.all_to_all(keys_out, "band", split_axis=0, concat_axis=0, tiled=True),
     )
     column_full = widen(arrived)

time: 188 us -> 203 us (1.080)
  starting transfers between devices: 19.2 us -> 26.1 us
  waiting for transfers between devices: 49.3 us -> 53.3 us
  local copies, waits for them, and re-layouts: 12.3 us -> 15.1 us
    ppermute x0 -> x7, starting transfers between devices: none -> 11.2 us  [exchange_in_pairs(): part = lax.ppermute(part, axis, [(d, d ^ mask) for d in range(ways)])]
    all_to_all x2, waiting for transfers between devices: 6.16 us -> 11.5 us  [move_rows(): return lax.all_to_all(rows, 'band', split_axis=0, concat_axis=0, tiled=True)]
    reduce_scatter x4, waiting for transfers between devices: 39.1 us -> 34.7 us  [narrow(): lax.psum_scatter(terms.astype(jnp.bfloat16), 'mp', scatter_dimension=1, t...]
    all_to_all x1 -> x0, starting transfers between devices: 4.31 us -> none  [on_device(): lax.all_to_all(outgoing, 'band', split_axis=0, concat_axis=0, tiled=True)]
    ppermute x0 -> x7, waiting for transfers between devices: none -> 3.11 us  [exchange_in_pairs(): part = lax.ppermute(part, axis, [(d, d ^ mask) for d in range(ways)])]
  transfers between devices with their start and end apart: 8 -> 14, of which waited for: 7 -> 8; matrix products, arithmetic and copies ran while one was open for 12% -> 11% of each run, Pallas kernels for 0% -> 0%
where the time goes in v1:
time: 203 us; the launch traced here: 202 us
  waiting for transfers between devices  53.3 us (26%)
  blocking collectives  45.6 us (22%)
  matrix products  35.1 us (17%)
  starting transfers between devices  26.1 us (13%)
  local copies, waits for them, and re-layouts  15.1 us (7%)
  between operations  14.3 us (7%)
  other arithmetic  12 us (6%)
    reduce_scatter x4, waiting for transfers between devices, narrow(): lax.psum_scatter(terms.astype(jnp.bfloat16), 'mp', scatter_dimension=1, t...  34.7 us
    all_gather x4, blocking collectives, widen(): return lax.all_gather(block, 'mp', axis=1, tiled=True)  32.3 us
    all_to_all x1, blocking collectives, move_rows(): return lax.all_to_all(rows, 'band', split_axis=0, concat_axis=0, tiled=True)  13.3 us
    all_to_all x2, waiting for transfers between devices, move_rows(): return lax.all_to_all(rows, 'band', split_axis=0, concat_axis=0, tiled=True)  11.5 us
    ppermute x7, starting transfers between devices, exchange_in_pairs(): part = lax.ppermute(part, axis, [(d, d ^ mask) for d in range(ways)])  11.2 us
    dot_general x6, matrix products, block_terms(): jnp.einsum('bhqk,bkhe->bqhe', attn_probs, shaped[2], preferred_element_ty...  11.1 us
    all_to_all x2, starting transfers between devices, move_rows(): return lax.all_to_all(rows, 'band', split_axis=0, concat_axis=0, tiled=True)  8.91 us
    dot_general x4, matrix products, block_terms(): jnp.einsum('bqhe,bkhe->bhqk', shaped[0], shaped[1], preferred_element_typ...  8.12 us
  transfers between devices with their start and end apart: 14, of which 8 were waited for; matrix products, arithmetic and copies ran while one was open for 11% of the time, Pallas kernels for 0%

profile of v1, /device:TPU:0, one launch (start us, length us, event | category | flops | bytes accessed | tf_op | source)
XLA Modules:
  0.0 201.5 jit_solution(16791798259761796322)
XLA Ops:
  7.2 9.0 %all_gather.12 = bf16[256,1024]{1,0:T(8,128)(2,1)S(1)} all-gather(bf16[256,256]{1,0:T(8,128)(2,1)} %param.11), channel_id=1, replica_groups=mesh['band'=8,'mp'=4] {'mp'}, dimensions={1}, use_global_device_ids=true | all-gather | bytes 655360 | tf_op jit(solution)/shard_map/all_gather | solution.py:60
  24.3 2.2 %scatter_custom_fusion.1 = bf16[384]{0:T(512)(128)(2,1)S(1)} fusion(s32[256]{0:T(256)S(1)} %bitcast.151, bf16[256]{0:T(256)(128)(2,1)S(1)} %convert_element_type.204, bf16[]{:T(256)} %constant.21.clone.1), kind=kCustom, calls=%fused_computation.136 | custom fusion | bytes 770 | tf_op jit(solution)/shard_map/scatter | solution.py:106
  27.1 5.8 %all-to-all-start = ((bf16[8,48,1]{1,2,0:T(2,128)(2,1)}), bf16[8,48,1]{1,2,0:T(2,128)(2,1)S(1)}, u32[]{:S(2)}, u32[]{:S(2)}) async-start(bf16[8,48,1]{1,2,0:T(2,128)(2,1)} %all_to_all.41), calls=%async_computation.1 | async-start | bytes 8192 | tf_op jit(solution)/shard_map/all_to_all | solution.py:113
  33.0 2.5 %scatter_custom_fusion.2 = bf16[384,256]{1,0:T(8,128)(2,1)} fusion(s32[256]{0:T(256)S(1)} %bitcast.152, bf16[256,256]{1,0:T(8,128)(2,1)} %param.21, bf16[]{:T(256)} %constant.21.clone.1), kind=kCustom, calls=%fused_computation.106 | custom fusion | bytes 197120 | tf_op jit(solution)/shard_map/scatter | solution.py:108
  35.4 4.0 %all-to-all-done = bf16[8,48,1]{1,2,0:T(2,128)(2,1)S(1)} async-done(((bf16[8,48,1]{1,2,0:T(2,128)(2,1)}), bf16[8,48,1]{1,2,0:T(2,128)(2,1)S(1)}, u32[]{:S(2)}, u32[]{:S(2)}) %all-to-all-start) | async-done | bytes 800 | tf_op jit(solution)/shard_map/all_to_all | solution.py:113
  39.4 3.4 %all-to-all-start.2 = ((bf16[8,48,256]{2,1,0:T(8,128)(2,1)}), bf16[8,48,256]{2,1,0:T(8,128)(2,1)S(1)}, u32[]{:S(2)}, u32[]{:S(2)}) async-start(bf16[8,48,256]{2,1,0:T(8,128)(2,1)} %bitcast.17), calls=%async_computation.4 | async-start | bytes 393216 | tf_op jit(solution)/shard_map/all_to_all | solution.py:70
  43.9 6.7 %all-to-all-done.2 = bf16[8,48,256]{2,1,0:T(8,128)(2,1)S(1)} async-done(((bf16[8,48,256]{2,1,0:T(8,128)(2,1)}), bf16[8,48,256]{2,1,0:T(8,128)(2,1)S(1)}, u32[]{:S(2)}, u32[]{:S(2)}) %all-to-all-start.2) | async-done | bytes 196640 | tf_op jit(solution)/shard_map/all_to_all | solution.py:70
  51.2 8.4 %all_gather.14 = bf16[384,1024]{1,0:T(8,128)(2,1)S(1)} all-gather(bf16[384,256]{1,0:T(8,128)(2,1)} %bitcast.133), channel_id=1, replica_groups=mesh['band'=8,'mp'=4] {'mp'}, dimensions={1}, use_global_device_ids=true | all-gather | bytes 983040 | tf_op jit(solution)/shard_map/all_gather | solution.py:60
  59.7 2.5 %scatter_custom_fusion = bf16[384,256]{1,0:T(8,128)(2,1)} fusion(s32[256]{0:T(256)S(1)} %bitcast.153, bf16[256,256]{1,0:T(8,128)(2,1)} %reduce-scatter.5.cloned.1.call-done, bf16[256,256]{1,0:T(8,128)(2,1)S(1)} %copy-done.13, bf16[]{:T(256)} %constant.21.clone.1), kind=kCustom, calls=%fused_computation.101 | custom fusion | flops 262144 | bytes 458754 | tf_op jit(solution)/shard_map/scatter | solution.py:110
  68.2 2.8 %collective-permute-start.4 = (bf16[48,256]{1,0:T(8,128)(2,1)S(1)}, bf16[48,256]{1,0:T(8,128)(2,1)S(1)}, u32[]{:S(2)}, u32[]{:S(2)}) collective-permute-start(bf16[48,256]{1,0:T(8,128)(2,1)S(1)} %get-tuple-element.12), channel_id=1, source_target_pairs={{0,20},{4,16},{8,28},{12,24},{16,4},{20,0},{24,12},{28,8},{1,21},{... | collective-permute-start | bytes 73736 | tf_op jit(solution)/shard_map/ppermute | solution.py:23
  72.1 3.4 %collective-permute-start.6 = (bf16[48,256]{1,0:T(8,128)(2,1)S(1)}, bf16[48,256]{1,0:T(8,128)(2,1)S(1)}, u32[]{:S(2)}, u32[]{:S(2)}) collective-permute-start(bf16[48,256]{1,0:T(8,128)(2,1)S(1)} %get-tuple-element.10), channel_id=1, source_target_pairs={{0,28},{4,24},{8,20},{12,16},{16,12},{20,8},{24,4},{28,0},{1,29},{... | collective-permute-start | bytes 73736 | tf_op jit(solution)/shard_map/ppermute | solution.py:23
  79.3 8.2 %all_gather.13 = bf16[384,1024]{1,0:T(8,128)(2,1)S(1)} all-gather(bf16[384,256]{1,0:T(8,128)(2,1)S(1)} %constant_dynamic-update-slice_fusion.6), channel_id=1, replica_groups=mesh['band'=8,'mp'=4] {'mp'}, dimensions={1}, use_global_device_ids=true | all-gather | bytes 983040 | tf_op jit(solution)/shard_map/all_gather | solution.py:60
  89.6 3.4 %fusion.74 = (f32[4,384]{1,0:T(4,128)S(1)}, f32[4,384,384]{1,2,0:T(8,128)}) fusion(pred[384,384]{0,1:T(8,128)(4,1)} %fusion.43, bf16[384,4,64]{0,2,1:T(8,128)(2,1)} %bitcast.146, bf16[384,4,64]{0,2,1:T(8,128)(2,1)S(1)} %bitcast.143), kind=kOutput, calls=%fused_computation.146 | convolution fusion | flops 77857152 | bytes 2906112 | tf_op jit(solution)/shard_map/jvp()/sub | solution.py:43
  93.0 3.7 %fusion.7 = (f32[4,384]{1,0:T(4,128)S(1)}, bf16[4,384,384]{1,2,0:T(8,128)(2,1)}, bf16[4,384,384]{1,2,0:T(8,128)(2,1)}) fusion(f32[4,384,384]{1,2,0:T(8,128)} %get-tuple-element.21, f32[4,384]{1,0:T(4,128)S(1)} %multiply_divide_fusion, f32[4,384]{1,0:T(4,128)S(1)} %get-tuple-element.20, bf16[4,64,384]{2,1,0:T(8,128)(2,1)S(1)} %bitcast.137, ...), kind=kOutput, calls=%fused_computation.19 | convolution fusion | flops 79624704 | bytes 5130240 | tf_op jit(solution)/shard_map/transpose(jvp(bhqk,bkhe->bqhe))/dot_general | solution.py:46
  96.7 3.9 %fusion.26 = bf16[1,1,384,4,64]{2,4,3,1,0:T(8,128)(2,1)} fusion(bf16[384,4,64]{0,2,1:T(8,128)(2,1)} %bitcast.147, bf16[4,384,384]{1,2,0:T(8,128)(2,1)} %get-tuple-element.22, f32[4,384]{1,0:T(4,128)S(1)} %neg.13, f32[4,384]{1,0:T(4,128)S(1)} %get-tuple-element.20, pred[384,384]{0,1:T(8,128)(4,1)} %fusion.43, bf16[384,4,64]{0,2,1:T(8,128)(2,1)S(1)} %bitcast.144), kind=kOutput, calls=%fused_computation.61 | convolution fusion | flops 156403584 | bytes 1929216 | tf_op jit(solution)/shard_map/transpose(jvp(bqhe,bkhe->bhqk))/dot_general | solution.py:39
  100.7 3.7 %fusion.27 = bf16[1,1,384,4,64]{2,4,3,1,0:T(8,128)(2,1)} fusion(bf16[384,4,64]{0,2,1:T(8,128)(2,1)S(1)} %bitcast.145, bf16[4,384,384]{1,2,0:T(8,128)(2,1)} %get-tuple-element.22, f32[4,384]{1,0:T(4,128)S(1)} %neg.13, f32[4,384]{1,0:T(4,128)S(1)} %get-tuple-element.20, pred[384,384]{0,1:T(8,128)(4,1)} %fusion.43, bf16[384,4,64]{0,2,1:T(8,128)(2,1)S(1)} %bitcast.148), kind=kOutput, calls=%fused_computation.62 | convolution fusion | flops 156403584 | bytes 1929216 | tf_op jit(solution)/shard_map/transpose(jvp(bqhe,bkhe->bhqk))/dot_general | solution.py:39
  111.7 23.0 %reduce-scatter.9.cloned.1.call-done = bf16[384,256]{1,0:T(8,128)(2,1)} async-done(((bf16[384,1024]{1,0:T(8,128)(2,1)}), bf16[384,256]{1,0:T(8,128)(2,1)}) %reduce-scatter.9.cloned.1.call-update) | async-done | bytes 196624 | tf_op jit(solution)/shard_map/reduce_scatter | solution.py:64
  136.5 5.5 %all-to-all-start.3 = ((bf16[8,48,256]{2,1,0:T(8,128)(2,1)}), bf16[8,48,256]{2,1,0:T(8,128)(2,1)S(1)}, u32[]{:S(2)}, u32[]{:S(2)}) async-start(bf16[8,48,256]{2,1,0:T(8,128)(2,1)} %bitcast.36), calls=%async_computation.6 | async-start | bytes 393216 | tf_op jit(solution)/shard_map/all_to_all | solution.py:70
  145.2 4.8 %all-to-all-done.3 = bf16[8,48,256]{2,1,0:T(8,128)(2,1)S(1)} async-done(((bf16[8,48,256]{2,1,0:T(8,128)(2,1)}), bf16[8,48,256]{2,1,0:T(8,128)(2,1)S(1)}, u32[]{:S(2)}, u32[]{:S(2)}) %all-to-all-start.3) | async-done | bytes 196640 | tf_op jit(solution)/shard_map/all_to_all | solution.py:70
  151.1 6.7 %all-gather = bf16[256,1024]{1,0:T(8,128)(2,1)S(1)} all-gather(bf16[256,256]{1,0:T(8,128)(2,1)S(1)} %gather_fusion.1), channel_id=2, replica_groups=mesh['band'=8,'mp'=4] {'mp'}, dimensions={1}, use_global_device_ids=true | all-gather | bytes 655360 | tf_op jit(solution)/shard_map/all_gather | solution.py:60
  162.5 2.1 %fusion.37 = (f32[256]{0:T(256)S(1)}, f32[256,1024]{1,0:T(8,128)S(1)}) fusion(bf16[256,1024]{1,0:T(8,128)(2,1)S(1)} %all_gather.12, f32[1024]{0:T(1024)S(1)} %copy-done.23, bf16[3,1024,256]{2,1,0:T(8,128)(2,1)} %param.13, bf16[3,256,256]{1,2,0:T(8,128)(2,1)S(1)} %reshape.260), kind=kOutput, calls=%fused_computation.77 | convolution fusion | flops 404225792 | bytes 3544064 | tf_op jit(solution)/shard_map/transpose(jvp(lu,xuh->xlh))/dot_general | solution.py:32
  165.7 3.5 %reduce-scatter.7.cloned.1.call-done = bf16[384,256]{1,0:T(8,128)(2,1)} async-done(((bf16[384,1024]{1,0:T(8,128)(2,1)}), bf16[384,256]{1,0:T(8,128)(2,1)}) %reduce-scatter.7.cloned.1.call-update) | async-done | bytes 196624 | tf_op jit(solution)/shard_map/reduce_scatter | solution.py:64
  170.2 13.3 %all_to_all.46 = bf16[8,48,256]{2,1,0:T(8,128)(2,1)S(1)} all-to-all(bf16[8,48,256]{2,1,0:T(8,128)(2,1)S(1)} %bitcast.136), channel_id=1, replica_groups=mesh['band'=8,'mp'=4] {'band'}, dimensions={0} | all-to-all | bytes 393216 | tf_op jit(solution)/shard_map/all_to_all | solution.py:70
  185.2 8.2 %reduce-scatter.11.cloned.1.call-done = bf16[256,256]{1,0:T(8,128)(2,1)} async-done(((bf16[256,1024]{1,0:T(8,128)(2,1)}), bf16[256,256]{1,0:T(8,128)(2,1)}) %reduce-scatter.11.cloned.1.call-update) | async-done | bytes 131088 | tf_op jit(solution)/shard_map/reduce_scatter | solution.py:64
  (144 shorter events, 46.6 us)
Async XLA Ops:
  7.2 80.5 %copy-start = (bf16[3,1024,256]{2,1,0:T(8,128)(2,1)S(1)}, bf16[3,1024,256]{2,1,0:T(8,128)(2,1)}, u32[]{:S(2)}) copy-start(bf16[3,1024,256]{2,1,0:T(8,128)(2,1)} %param.16) | copy-start | bytes 4718596
  7.2 52.5 %reduce-scatter.5.cloned.1.call-start = ((), (), s32[]{:S(2)}) async-start(), calls=%async_computation.8 | async-start | bytes 655360 | tf_op jit(solution)/shard_map/reduce_scatter | solution.py:64
  19.7 4.4 %copy-start.21 = (s32[256,1]{0,1:T(1,128)S(1)}, s32[256,1]{0,1:T(1,128)}, u32[]{:S(2)}) copy-start(s32[256,1]{0,1:T(1,128)} %param.19) | copy-start | bytes 3076
  22.7 36.9 %copy-start.13 = (bf16[256,256]{1,0:T(8,128)(2,1)S(1)}, bf16[256,256]{1,0:T(8,128)(2,1)}, u32[]{:S(2)}) copy-start(bf16[256,256]{1,0:T(8,128)(2,1)} %param.11) | copy-start | bytes 393220
  22.9 41.1 %copy-start.1 = (bf16[256,1024]{1,0:T(8,128)(2,1)S(1)}, bf16[256,1024]{1,0:T(8,128)(2,1)}, u32[]{:S(2)}) copy-start(bf16[256,1024]{1,0:T(8,128)(2,1)} %param.17) | copy-start | bytes 1572868
  27.1 12.3 %all-to-all-start = ((bf16[8,48,1]{1,2,0:T(2,128)(2,1)}), bf16[8,48,1]{1,2,0:T(2,128)(2,1)S(1)}, u32[]{:S(2)}, u32[]{:S(2)}) async-start(bf16[8,48,1]{1,2,0:T(2,128)(2,1)} %all_to_all.41), calls=%async_computation.1 | async-start | bytes 8192 | tf_op jit(solution)/shard_map/all_to_all | solution.py:113
  39.4 11.1 %all-to-all-start.2 = ((bf16[8,48,256]{2,1,0:T(8,128)(2,1)}), bf16[8,48,256]{2,1,0:T(8,128)(2,1)S(1)}, u32[]{:S(2)}, u32[]{:S(2)}) async-start(bf16[8,48,256]{2,1,0:T(8,128)(2,1)} %bitcast.17), calls=%async_computation.4 | async-start | bytes 393216 | tf_op jit(solution)/shard_map/all_to_all | solution.py:70
  42.8 91.9 %reduce-scatter.9.cloned.1.call-start = ((), (), s32[]{:S(2)}) async-start(), calls=%async_computation.10 | async-start | bytes 983040 | tf_op jit(solution)/shard_map/reduce_scatter | solution.py:64
  59.6 28.1 %copy-start.22 = (f32[1024]{0:T(1024)S(1)}, f32[1024]{0:T(1024)}, u32[]{:S(2)}) copy-start(f32[1024]{0:T(1024)} %param.15) | copy-start | bytes 12292
  63.1 7.9 %collective-permute-start = (bf16[48,256]{1,0:T(8,128)(2,1)S(1)}, bf16[48,256]{1,0:T(8,128)(2,1)S(1)}, u32[]{:S(2)}, u32[]{:S(2)}) collective-permute-start(bf16[48,256]{1,0:T(8,128)(2,1)S(1)} %get-tuple-element.16), channel_id=1, source_target_pairs={{0,4},{4,0},{8,12},{12,8},{16,20},{20,16},{24,28},{28,24},{1,5},{5... | collective-permute-start | bytes 73736 | tf_op jit(solution)/shard_map/ppermute | solution.py:23
  65.1 6.9 %collective-permute-start.1 = (bf16[48,256]{1,0:T(8,128)(2,1)S(1)}, bf16[48,256]{1,0:T(8,128)(2,1)S(1)}, u32[]{:S(2)}, u32[]{:S(2)}) collective-permute-start(bf16[48,256]{1,0:T(8,128)(2,1)S(1)} %get-tuple-element.15), channel_id=1, source_target_pairs={{0,8},{4,12},{8,0},{12,4},{16,24},{20,28},{24,16},{28,20},{1,9},{5... | collective-permute-start | bytes 73736 | tf_op jit(solution)/shard_map/ppermute | solution.py:23
  65.7 9.8 %collective-permute-start.2 = (bf16[48,256]{1,0:T(8,128)(2,1)S(1)}, bf16[48,256]{1,0:T(8,128)(2,1)S(1)}, u32[]{:S(2)}, u32[]{:S(2)}) collective-permute-start(bf16[48,256]{1,0:T(8,128)(2,1)S(1)} %get-tuple-element.14), channel_id=1, source_target_pairs={{0,12},{4,8},{8,4},{12,0},{16,28},{20,24},{24,20},{28,16},{1,13},{... | collective-permute-start | bytes 73736 | tf_op jit(solution)/shard_map/ppermute | solution.py:23
  67.7 7.7 %collective-permute-start.3 = (bf16[48,256]{1,0:T(8,128)(2,1)S(1)}, bf16[48,256]{1,0:T(8,128)(2,1)S(1)}, u32[]{:S(2)}, u32[]{:S(2)}) collective-permute-start(bf16[48,256]{1,0:T(8,128)(2,1)S(1)} %get-tuple-element.13), channel_id=1, source_target_pairs={{0,16},{4,20},{8,24},{12,28},{16,0},{20,4},{24,8},{28,12},{1,17},{... | collective-permute-start | bytes 73736 | tf_op jit(solution)/shard_map/ppermute | solution.py:23
  68.2 7.2 %collective-permute-start.4 = (bf16[48,256]{1,0:T(8,128)(2,1)S(1)}, bf16[48,256]{1,0:T(8,128)(2,1)S(1)}, u32[]{:S(2)}, u32[]{:S(2)}) collective-permute-start(bf16[48,256]{1,0:T(8,128)(2,1)S(1)} %get-tuple-element.12), channel_id=1, source_target_pairs={{0,20},{4,16},{8,28},{12,24},{16,4},{20,0},{24,12},{28,8},{1,21},{... | collective-permute-start | bytes 73736 | tf_op jit(solution)/shard_map/ppermute | solution.py:23
  71.0 5.6 %collective-permute-start.5 = (bf16[48,256]{1,0:T(8,128)(2,1)S(1)}, bf16[48,256]{1,0:T(8,128)(2,1)S(1)}, u32[]{:S(2)}, u32[]{:S(2)}) collective-permute-start(bf16[48,256]{1,0:T(8,128)(2,1)S(1)} %get-tuple-element.11), channel_id=1, source_target_pairs={{0,24},{4,28},{8,16},{12,20},{16,8},{20,12},{24,0},{28,4},{1,25},{... | collective-permute-start | bytes 73736 | tf_op jit(solution)/shard_map/ppermute | solution.py:23
  72.1 6.5 %collective-permute-start.6 = (bf16[48,256]{1,0:T(8,128)(2,1)S(1)}, bf16[48,256]{1,0:T(8,128)(2,1)S(1)}, u32[]{:S(2)}, u32[]{:S(2)}) collective-permute-start(bf16[48,256]{1,0:T(8,128)(2,1)S(1)} %get-tuple-element.10), channel_id=1, source_target_pairs={{0,28},{4,24},{8,20},{12,16},{16,12},{20,8},{24,4},{28,0},{1,29},{... | collective-permute-start | bytes 73736 | tf_op jit(solution)/shard_map/ppermute | solution.py:23
  89.6 7.2 %copy-start.8 = (bf16[1,384,256]{1,2,0:T(8,128)(2,1)}, bf16[1,384,256]{1,2,0:T(8,128)(2,1)S(1)}, u32[]{:S(2)}) copy-start(bf16[1,384,256]{1,2,0:T(8,128)(2,1)S(1)} %get-tuple-element.6) | copy-start | bytes 589828
  110.3 33.5 %copy-start.2 = (bf16[256,1024]{1,0:T(8,128)(2,1)S(1)}, bf16[256,1024]{1,0:T(8,128)(2,1)}, u32[]{:S(2)}) copy-start(bf16[256,1024]{1,0:T(8,128)(2,1)} %param.17) | copy-start | bytes 1572868
  136.5 13.5 %all-to-all-start.3 = ((bf16[8,48,256]{2,1,0:T(8,128)(2,1)}), bf16[8,48,256]{2,1,0:T(8,128)(2,1)S(1)}, u32[]{:S(2)}, u32[]{:S(2)}) async-start(bf16[8,48,256]{2,1,0:T(8,128)(2,1)} %bitcast.36), calls=%async_computation.6 | async-start | bytes 393216 | tf_op jit(solution)/shard_map/all_to_all | solution.py:70
  142.0 27.2 %reduce-scatter.7.cloned.1.call-start = ((), (), s32[]{:S(2)}) async-start(), calls=%async_computation.9 | async-start | bytes 983040 | tf_op jit(solution)/shard_map/reduce_scatter | solution.py:64
  143.8 14.1 %copy-start.4 = (bf16[256,1024]{1,0:T(8,128)(2,1)S(1)}, bf16[256,1024]{1,0:T(8,128)(2,1)}, u32[]{:S(2)}) copy-start(bf16[256,1024]{1,0:T(8,128)(2,1)} %param.14) | copy-start | bytes 1572868
  145.1 13.3 %copy-start.11 = (bf16[2,128,4,64]{1,3,2,0:T(8,128)(2,1)S(1)}, bf16[2,128,4,64]{1,3,2,0:T(8,128)(2,1)}, u32[]{:S(2)}) copy-start(bf16[2,128,4,64]{1,3,2,0:T(8,128)(2,1)} %copy-done.10) | copy-start | bytes 393220
  145.1 48.3 %reduce-scatter.11.cloned.1.call-start = ((), (), s32[]{:S(2)}) async-start(), calls=%async_computation.11 | async-start | bytes 655360 | tf_op jit(solution)/shard_map/reduce_scatter | solution.py:64
  162.4 6.7 %copy-start.7 = (bf16[384,256]{1,0:T(8,128)(2,1)S(1)}, bf16[384,256]{1,0:T(8,128)(2,1)}, u32[]{:S(2)}) copy-start(bf16[384,256]{1,0:T(8,128)(2,1)} %copy-done.6) | copy-start | bytes 589828
  (18 other events, 46.2 us)
Sparse Core Ops, SparseCore 0:
  24.2 22.5 reduce-scatter.4
  111.8 22.9 reduce-scatter.8
  145.4 23.7 reduce-scatter.6
  171.7 21.6 reduce-scatter.10
